TPU v7x, 256 devices: a whole 4x4x8 slice. The times are simulated.
256 devices in a mesh: row: 64 (over z, x, core), col: 4 (over y).
Axes of the slice: x: 4, y: 4, z: 8, core: 2. Of those that a mesh axis runs over, the one named last changes fastest.
Arguments:
- hamiltonian: bfloat16 [18432, 128, 128], P('row'), may hold values from -0.15625 to 0.15625
- block_column: int32 [18432], P('row'), may hold values from 0 to 1535, as said below
- vectors: bfloat16 [196608, 512], P('row', 'col'), may hold values from -6 to 6
Outputs:
- filtered: bfloat16 [196608, 512], P('row', 'col')
- intersection: float32 [512, 512], P('col')
Inputs may be any that keep to these rules, and one draw needn't show every extreme that they name: Block row b's entries are block_column[b * 12 + k]. Entry k = 0 is b itself. Entries k < 10 are distinct and lie among the 24 block rows of b's own index of row (block rows i * 24 to i * 24 + 23 for i = b // 24). For k >= 10, let s = (b % 24) * 2 + k - 10 and g = s // 12; the entry lies among the block rows of index (i + o) mod 64, with o = g + 1 if g < 2, else 2 - 1 - g.
All inputs are finite; a program needn't handle non-finite values.
Results may differ from a plain program's by a relative error of at most 0.0056.
Values may be sent and summed in bfloat16 or wider, within the bound.
A program may use at most 192 MiB of HBM per device.

v0:
```python
import jax
import jax.numpy as jnp
from jax import lax
from jax.sharding import PartitionSpec as P

RPR = 2
REACH = 2
STEPS = 3
filter_center = 0.2
filter_half = 0.8


def from_behind(block, axis, distance):
    devices = range(lax.axis_size(axis))
    route = [((i - distance) % len(devices), i) for i in devices]
    return lax.ppermute(block, axis, route)


def on_device(hamiltonian, block_column, vectors):
    block_size = hamiltonian.shape[1]
    row_count = vectors.shape[0] // block_size
    width_dev = vectors.shape[1]
    per_row = hamiltonian.shape[0] // row_count
    local_count = per_row - RPR
    devices = lax.axis_size("row")
    capacity = RPR * row_count // (2 * REACH)
    offsets = [number + 1 for number in range(REACH)] + [-(number + 1) for number in range(REACH)]
    matrix_rows = hamiltonian.reshape(row_count, per_row, block_size, block_size)
    columns = block_column.reshape(row_count, per_row) % row_count
    local_index = columns[:, :local_count]
    wanted = columns[:, local_count:].reshape(2 * REACH, capacity)
    spread = jnp.arange(2 * REACH * capacity) // capacity * row_count + wanted.reshape(-1)
    remote_index = spread.reshape(row_count, RPR)

    def fetch_remote(blocks):
        stacked = jnp.concatenate(
            [from_behind(blocks, "row", -offset) for offset in offsets], axis=0
        )
        return stacked[remote_index]

    def operate(blocks):
        remote = fetch_remote(blocks)
        gathered = jnp.concatenate([blocks[local_index], remote], axis=1)
        return jnp.einsum(
            "rqij,rqjk->rik", matrix_rows, gathered, preferred_element_type=jnp.float32
        )

    previous = vectors.reshape(row_count, block_size, width_dev)
    current = (
        (operate(previous) - filter_center * previous.astype(jnp.float32)) / filter_half
    ).astype(jnp.bfloat16)
    for section in range(STEPS - 1):
        product = operate(current)
        following = (
            2.0 * (product - filter_center * current.astype(jnp.float32)) / filter_half
            - previous.astype(jnp.float32)
        ).astype(jnp.bfloat16)
        previous, current = (current, following)
    filtered = current.reshape(row_count * block_size, width_dev)
    partial_value = lax.dot_general(
        filtered,
        lax.all_gather(filtered, "col", axis=1, tiled=True),
        (((0,), (0,)), ((), ())),
        preferred_element_type=jnp.float32,
    )
    summed = lax.psum(partial_value, "row")
    return (filtered, summed / (devices * row_count * block_size))


def solution(mesh):
    return jax.shard_map(
        on_device,
        mesh=mesh,
        in_specs=(P("row", None, None), P("row"), P("row", "col")),
        out_specs=(P("row", "col"), P("col", None)),
        check_vma=False,
    )
```

profile of v0, /device:TPU:1, one launch (start us, length us, event | category | flops | bytes accessed | tf_op | source)
XLA Modules:
  0.0 386.9 jit_solution(11213303579981072683)
XLA Ops:
  7.2 2.1 collective-permute-start.3
  9.3 2.1 collective-permute-start.2
  11.4 4.7 %collective-permute-start.1 = (bf16[24,128,128]{2,1,0:T(8,128)(2,1)}, bf16[24,128,128]{2,1,0:T(8,128)(2,1)S(1)}, u32[]{:S(2)}, u32[]{:S(2)}) collective-permute-start(bf16[24,128,128]{2,1,0:T(8,128)(2,1)} %bitcast.35), channel_id=1, source_target_pairs={{8,0},{12,4},{16,8},{20,12},{24,16},{28,20},{32,24},{36,28},{40,32... | collective-permute-start | bytes 2359304 | tf_op jit(solution)/shard_map/ppermute | solution.py:16
  16.1 1.0 collective-permute-start
  18.1 9.6 %gather_fusion = bf16[240,128,128]{2,1,0:T(8,128)(2,1)} fusion(bf16[24,128,128]{2,1,0:T(8,128)(2,1)} %bitcast.37, s32[1024]{0:T(1024)S(1)} %pad_clamp_fusion.1), kind=kCustom, calls=%fused_computation | custom fusion | bytes 15729600 | tf_op jit(solution)/shard_map/gather | solution.py:43
  27.7 5.7 %collective-permute-done.3 = bf16[24,128,128]{2,1,0:T(8,128)(2,1)S(1)} collective-permute-done((bf16[24,128,128]{2,1,0:T(8,128)(2,1)}, bf16[24,128,128]{2,1,0:T(8,128)(2,1)S(1)}, u32[]{:S(2)}, u32[]{:S(2)}) %collective-permute-start.3) | collective-permute-done | bytes 786464 | tf_op jit(solution)/shard_map/ppermute | solution.py:16
  33.4 2.1 collective-permute-done.2
  35.4 3.9 %collective-permute-done = bf16[24,128,128]{2,1,0:T(8,128)(2,1)S(1)} collective-permute-done((bf16[24,128,128]{2,1,0:T(8,128)(2,1)}, bf16[24,128,128]{2,1,0:T(8,128)(2,1)S(1)}, u32[]{:S(2)}, u32[]{:S(2)}) %collective-permute-start) | collective-permute-done | bytes 786464 | tf_op jit(solution)/shard_map/ppermute | solution.py:16
  39.4 1.9 pad_maximum_fusion
  41.3 2.8 gather_fusion.1
  44.1 8.5 %fusion.14 = bf16[24,128,128]{2,1,0:T(8,128)(2,1)S(1)} fusion(bf16[24,128,128]{2,1,0:T(8,128)(2,1)S(1)} %bitcast.38, bf16[24,12,128,128]{3,2,1,0:T(8,128)(2,1)} %bitcast.49, bf16[24,2,128,128]{3,2,1,0:T(8,128)(2,1)S(1)} %bitcast.47, bf16[24,10,128,128]{3,2,1,0:T(8,128)(2,1)} %bitcast.41), kind=kOutput, calls=%fused_computation.27 | convolution fusion | flops 1228800000 | bytes 20447232 | tf_op jit(solution)/shard_map/rqij,rqjk->rik/dot_general | solution.py:44
  53.5 7.7 %collective-permute-start.5 = (bf16[24,128,128]{2,1,0:T(8,128)(2,1)S(1)}, bf16[24,128,128]{2,1,0:T(8,128)(2,1)}, u32[]{:S(2)}, u32[]{:S(2)}) collective-permute-start(bf16[24,128,128]{2,1,0:T(8,128)(2,1)S(1)} %fusion.14), channel_id=1, source_target_pairs={{8,0},{12,4},{16,8},{20,12},{24,16},{28,20},{32,24},{36,28},{40,32... | collective-permute-start | bytes 2359304 | tf_op jit(solution)/shard_map/ppermute | solution.py:16
  61.8 8.4 %gather_fusion.2 = bf16[240,128,128]{2,1,0:T(8,128)(2,1)} fusion(bf16[24,128,128]{2,1,0:T(8,128)(2,1)S(1)} %fusion.14, s32[1024]{0:T(1024)S(1)} %pad_clamp_fusion.1), kind=kCustom, calls=%fused_computation.2 | custom fusion | bytes 15729600 | tf_op jit(solution)/shard_map/gather | solution.py:43
  70.2 7.6 %collective-permute-done.7 = bf16[24,128,128]{2,1,0:T(8,128)(2,1)S(1)} collective-permute-done((bf16[24,128,128]{2,1,0:T(8,128)(2,1)S(1)}, bf16[24,128,128]{2,1,0:T(8,128)(2,1)S(1)}, u32[]{:S(2)}, u32[]{:S(2)}) %collective-permute-start.7) | collective-permute-done | bytes 786464 | tf_op jit(solution)/shard_map/ppermute | solution.py:16
  77.8 1.2 collective-permute-done.6
  79.0 2.4 collective-permute-done.4
  81.4 3.0 pad_maximum_fusion.1
  84.5 3.9 gather_fusion.3
  88.4 9.0 %fusion.15 = bf16[24,128,128]{2,1,0:T(8,128)(2,1)S(1)} fusion(bf16[24,128,128]{2,1,0:T(8,128)(2,1)S(1)} %bitcast.39, bf16[24,128,128]{2,1,0:T(8,128)(2,1)S(1)} %fusion.14, bf16[24,12,128,128]{3,2,1,0:T(8,128)(2,1)} %bitcast.50, bf16[24,2,128,128]{3,2,1,0:T(8,128)(2,1)} %bitcast.48, bf16[24,10,128,128]{3,2,1,0:T(8,128)(2,1)} %bitcast.42), kind=kOutput, calls=%fused_computation.28 | convolution fusion | flops 1229586432 | bytes 21233664 | tf_op jit(solution)/shard_map/rqij,rqjk->rik/dot_general | solution.py:44
  97.4 3.0 collective-permute-start.11
  100.4 8.1 %collective-permute-start.9 = (bf16[24,128,128]{2,1,0:T(8,128)(2,1)S(1)}, bf16[24,128,128]{2,1,0:T(8,128)(2,1)}, u32[]{:S(2)}, u32[]{:S(2)}) collective-permute-start(bf16[24,128,128]{2,1,0:T(8,128)(2,1)S(1)} %fusion.15), channel_id=1, source_target_pairs={{8,0},{12,4},{16,8},{20,12},{24,16},{28,20},{32,24},{36,28},{40,32... | collective-permute-start | bytes 2359304 | tf_op jit(solution)/shard_map/ppermute | solution.py:16
  108.5 0.7 collective-permute-start.8
  109.2 8.4 %gather_fusion.4 = bf16[240,128,128]{2,1,0:T(8,128)(2,1)} fusion(bf16[24,128,128]{2,1,0:T(8,128)(2,1)S(1)} %fusion.15, s32[1024]{0:T(1024)S(1)} %pad_clamp_fusion.1), kind=kCustom, calls=%fused_computation.4 | custom fusion | bytes 15729600 | tf_op jit(solution)/shard_map/gather | solution.py:43
  117.6 8.3 %collective-permute-done.11 = bf16[24,128,128]{2,1,0:T(8,128)(2,1)S(1)} collective-permute-done((bf16[24,128,128]{2,1,0:T(8,128)(2,1)S(1)}, bf16[24,128,128]{2,1,0:T(8,128)(2,1)S(1)}, u32[]{:S(2)}, u32[]{:S(2)}) %collective-permute-start.11) | collective-permute-done | bytes 786464 | tf_op jit(solution)/shard_map/ppermute | solution.py:16
  126.2 2.2 collective-permute-done.8
  128.4 3.0 pad_maximum_fusion.2
  131.4 3.9 gather_fusion.5
  135.3 9.9 %fusion.18 = bf16[24,128,128]{2,1,0:T(8,128)(2,1)} fusion(bf16[24,128,128]{2,1,0:T(8,128)(2,1)S(1)} %fusion.14, bf16[24,128,128]{2,1,0:T(8,128)(2,1)S(1)} %fusion.15, bf16[24,12,128,128]{3,2,1,0:T(8,128)(2,1)} %bitcast.51, bf16[24,2,128,128]{3,2,1,0:T(8,128)(2,1)} %bitcast.46, bf16[24,10,128,128]{3,2,1,0:T(8,128)(2,1)} %bitcast.40), kind=kOutput, calls=%fused_computation.31 | convolution fusion | flops 1229586432 | bytes 21233664 | tf_op jit(solution)/shard_map/rqij,rqjk->rik/dot_general | solution.py:44
  145.2 52.0 %all-gather.2.cloned.1.call-done = bf16[3072,512]{1,0:T(8,128)(2,1)} async-done(((bf16[3072,128]{1,0:T(8,128)(2,1)}), bf16[3072,512]{1,0:T(8,128)(2,1)}) %all-gather.2.cloned.1.call-update) | async-done | bytes 3145744 | tf_op jit(solution)/shard_map/all_gather | solution.py:62
  197.2 3.5 fusion.32
  200.7 177.7 %all-reduce.2.cloned.1.call-done = f32[128,512]{1,0:T(8,128)} async-done(((f32[128,512]{1,0:T(8,128)}), f32[128,512]{1,0:T(8,128)}) %all-reduce.2.cloned.1.call-update) | async-done | bytes 262160 | tf_op jit(solution)/shard_map/psum | solution.py:66
  378.4 1.7 broadcast_multiply_fusion
  (23 shorter events, 2.8 us)
Async XLA Ops:
  7.2 190.0 %all-gather.2.cloned.1.call-start = ((), (), s32[]{:S(2)}) async-start(), calls=%async_computation | async-start | bytes 3932160 | tf_op jit(solution)/shard_map/all_gather | solution.py:62
  7.2 26.2 %collective-permute-start.3 = (bf16[24,128,128]{2,1,0:T(8,128)(2,1)}, bf16[24,128,128]{2,1,0:T(8,128)(2,1)S(1)}, u32[]{:S(2)}, u32[]{:S(2)}) collective-permute-start(bf16[24,128,128]{2,1,0:T(8,128)(2,1)} %bitcast.33), channel_id=1, source_target_pairs={{248,0},{252,4},{0,8},{4,12},{8,16},{12,20},{16,24},{20,28},{24,32... | collective-permute-start | bytes 2359304 | tf_op jit(solution)/shard_map/ppermute | solution.py:16
  9.3 26.1 %collective-permute-start.2 = (bf16[24,128,128]{2,1,0:T(8,128)(2,1)}, bf16[24,128,128]{2,1,0:T(8,128)(2,1)S(1)}, u32[]{:S(2)}, u32[]{:S(2)}) collective-permute-start(bf16[24,128,128]{2,1,0:T(8,128)(2,1)} %bitcast.34), channel_id=1, source_target_pairs={{252,0},{0,4},{4,8},{8,12},{12,16},{16,20},{20,24},{24,28},{28,32}... | collective-permute-start | bytes 2359304 | tf_op jit(solution)/shard_map/ppermute | solution.py:16
  11.4 24.1 %collective-permute-start.1 = (bf16[24,128,128]{2,1,0:T(8,128)(2,1)}, bf16[24,128,128]{2,1,0:T(8,128)(2,1)S(1)}, u32[]{:S(2)}, u32[]{:S(2)}) collective-permute-start(bf16[24,128,128]{2,1,0:T(8,128)(2,1)} %bitcast.35), channel_id=1, source_target_pairs={{8,0},{12,4},{16,8},{20,12},{24,16},{28,20},{32,24},{36,28},{40,32... | collective-permute-start | bytes 2359304 | tf_op jit(solution)/shard_map/ppermute | solution.py:16
  16.1 23.3 %collective-permute-start = (bf16[24,128,128]{2,1,0:T(8,128)(2,1)}, bf16[24,128,128]{2,1,0:T(8,128)(2,1)S(1)}, u32[]{:S(2)}, u32[]{:S(2)}) collective-permute-start(bf16[24,128,128]{2,1,0:T(8,128)(2,1)} %bitcast.36), channel_id=1, source_target_pairs={{4,0},{8,4},{12,8},{16,12},{20,16},{24,20},{28,24},{32,28},{36,32}... | collective-permute-start | bytes 2359304 | tf_op jit(solution)/shard_map/ppermute | solution.py:16
  41.3 2.8 copy-start
  52.7 25.1 %collective-permute-start.7 = (bf16[24,128,128]{2,1,0:T(8,128)(2,1)S(1)}, bf16[24,128,128]{2,1,0:T(8,128)(2,1)S(1)}, u32[]{:S(2)}, u32[]{:S(2)}) collective-permute-start(bf16[24,128,128]{2,1,0:T(8,128)(2,1)S(1)} %fusion.14), channel_id=1, source_target_pairs={{248,0},{252,4},{0,8},{4,12},{8,16},{12,20},{16,24},{20,28},{24,32... | collective-permute-start | bytes 2359304 | tf_op jit(solution)/shard_map/ppermute | solution.py:16
  53.2 25.8 %collective-permute-start.6 = (bf16[24,128,128]{2,1,0:T(8,128)(2,1)S(1)}, bf16[24,128,128]{2,1,0:T(8,128)(2,1)S(1)}, u32[]{:S(2)}, u32[]{:S(2)}) collective-permute-start(bf16[24,128,128]{2,1,0:T(8,128)(2,1)S(1)} %fusion.14), channel_id=1, source_target_pairs={{252,0},{0,4},{4,8},{8,12},{12,16},{16,20},{20,24},{24,28},{28,32}... | collective-permute-start | bytes 2359304 | tf_op jit(solution)/shard_map/ppermute | solution.py:16
  53.5 25.6 %collective-permute-start.5 = (bf16[24,128,128]{2,1,0:T(8,128)(2,1)S(1)}, bf16[24,128,128]{2,1,0:T(8,128)(2,1)}, u32[]{:S(2)}, u32[]{:S(2)}) collective-permute-start(bf16[24,128,128]{2,1,0:T(8,128)(2,1)S(1)} %fusion.14), channel_id=1, source_target_pairs={{8,0},{12,4},{16,8},{20,12},{24,16},{28,20},{32,24},{36,28},{40,32... | collective-permute-start | bytes 2359304 | tf_op jit(solution)/shard_map/ppermute | solution.py:16
  61.2 20.3 %collective-permute-start.4 = (bf16[24,128,128]{2,1,0:T(8,128)(2,1)S(1)}, bf16[24,128,128]{2,1,0:T(8,128)(2,1)}, u32[]{:S(2)}, u32[]{:S(2)}) collective-permute-start(bf16[24,128,128]{2,1,0:T(8,128)(2,1)S(1)} %fusion.14), channel_id=1, source_target_pairs={{4,0},{8,4},{12,8},{16,12},{20,16},{24,20},{28,24},{32,28},{36,32}... | collective-permute-start | bytes 2359304 | tf_op jit(solution)/shard_map/ppermute | solution.py:16
  97.4 28.5 %collective-permute-start.11 = (bf16[24,128,128]{2,1,0:T(8,128)(2,1)S(1)}, bf16[24,128,128]{2,1,0:T(8,128)(2,1)S(1)}, u32[]{:S(2)}, u32[]{:S(2)}) collective-permute-start(bf16[24,128,128]{2,1,0:T(8,128)(2,1)S(1)} %fusion.15), channel_id=1, source_target_pairs={{248,0},{252,4},{0,8},{4,12},{8,16},{12,20},{16,24},{20,28},{24,32... | collective-permute-start | bytes 2359304 | tf_op jit(solution)/shard_map/ppermute | solution.py:16
  100.4 25.8 %collective-permute-start.10 = (bf16[24,128,128]{2,1,0:T(8,128)(2,1)S(1)}, bf16[24,128,128]{2,1,0:T(8,128)(2,1)S(1)}, u32[]{:S(2)}, u32[]{:S(2)}) collective-permute-start(bf16[24,128,128]{2,1,0:T(8,128)(2,1)S(1)} %fusion.15), channel_id=1, source_target_pairs={{252,0},{0,4},{4,8},{8,12},{12,16},{16,20},{20,24},{24,28},{28,32}... | collective-permute-start | bytes 2359304 | tf_op jit(solution)/shard_map/ppermute | solution.py:16
  100.4 25.8 %collective-permute-start.9 = (bf16[24,128,128]{2,1,0:T(8,128)(2,1)S(1)}, bf16[24,128,128]{2,1,0:T(8,128)(2,1)}, u32[]{:S(2)}, u32[]{:S(2)}) collective-permute-start(bf16[24,128,128]{2,1,0:T(8,128)(2,1)S(1)} %fusion.15), channel_id=1, source_target_pairs={{8,0},{12,4},{16,8},{20,12},{24,16},{28,20},{32,24},{36,28},{40,32... | collective-permute-start | bytes 2359304 | tf_op jit(solution)/shard_map/ppermute | solution.py:16
  108.5 19.9 %collective-permute-start.8 = (bf16[24,128,128]{2,1,0:T(8,128)(2,1)S(1)}, bf16[24,128,128]{2,1,0:T(8,128)(2,1)}, u32[]{:S(2)}, u32[]{:S(2)}) collective-permute-start(bf16[24,128,128]{2,1,0:T(8,128)(2,1)S(1)} %fusion.15), channel_id=1, source_target_pairs={{4,0},{8,4},{12,8},{16,12},{20,16},{24,20},{28,24},{32,28},{36,32}... | collective-permute-start | bytes 2359304 | tf_op jit(solution)/shard_map/ppermute | solution.py:16
  145.2 233.2 %all-reduce.2.cloned.1.call-start = ((), (), s32[]{:S(2)}) async-start(), calls=%async_computation.1 | async-start | bytes 524288 | tf_op jit(solution)/shard_map/psum | solution.py:66
Sparse Core Ops, SparseCore 0:
  145.3 51.8 all-gather.1
  201.3 177.0 all-reduce.1
where the time goes:
time: 387 us
  waiting for transfers between devices  263 us (68%)
  local copies, waits for them, and re-layouts  37.2 us (10%)
  matrix products  30.9 us (8%)
  starting transfers between devices  30.8 us (8%)
  between operations  14.1 us (4%)
  other arithmetic  10.5 us (3%)
    psum x1, waiting for transfers between devices, on_device(): summed = lax.psum(partial_value, 'row')  178 us
    all_gather x1, waiting for transfers between devices, on_device(): lax.all_gather(filtered, 'col', axis=1, tiled=True)  52 us
    ppermute x12, waiting for transfers between devices, from_behind(): return lax.ppermute(block, axis, route)  33.7 us
    ppermute x12, starting transfers between devices, from_behind(): return lax.ppermute(block, axis, route)  30.7 us
    dot_general x3, matrix products, operate(): jnp.einsum('rqij,rqjk->rik', matrix_rows, gathered, preferred_element_typ...  27.4 us
    gather x3, local copies, waits for them, and re-layouts, operate(): gathered = jnp.concatenate([blocks[local_index], remote], axis=1)  26.4 us
    gather x3, local copies, waits for them, and re-layouts, fetch_remote(): return stacked[remote_index]  10.5 us
    concatenate x3, other arithmetic, fetch_remote(): jnp.concatenate([from_behind(blocks, 'row', -offset) for offset in offset...  8.01 us
  transfers between devices with their start and end apart: 14, of which 11 were waited for; matrix products, arithmetic and copies ran while one was open for 7% of the time, Pallas kernels for 0%

commit v1 on v0

--- a/solution.py
+++ b/solution.py
@@ -63,7 +63,7 @@
         (((0,), (0,)), ((), ())),
         preferred_element_type=jnp.float32,
     )
-    summed = lax.psum(partial_value, "row")
+    summed = jnp.sum(lax.all_gather(partial_value, "row"), axis=0)
     return (filtered, summed / (devices * row_count * block_size))
 
 

time: 387 us -> 318 us (0.82)
  waiting for transfers between devices: 263 us -> 188 us
  other arithmetic: 10.5 us -> 17.1 us
    psum x1 -> x0, waiting for transfers between devices: 178 us -> none  [on_device(): summed = lax.psum(partial_value, 'row')]
    all_gather x0 -> x1, waiting for transfers between devices: none -> 102 us  [on_device(): summed = jnp.sum(lax.all_gather(partial_value, 'row'), axis=0)]
    reduce_sum x0 -> x1, other arithmetic: none -> 7.52 us  [on_device(): summed = jnp.sum(lax.all_gather(partial_value, 'row'), axis=0)]
  transfers between devices with their start and end apart: 14 -> 14, of which waited for: 11 -> 11; matrix products, arithmetic and copies ran while one was open for 7% -> 9% of each run, Pallas kernels for 0% -> 0%
where the time goes in v1:
time: 318 us
  waiting for transfers between devices  188 us (59%)
  local copies, waits for them, and re-layouts  37.2 us (12%)
  matrix products  30.9 us (10%)
  starting transfers between devices  30.8 us (10%)
  other arithmetic  17.1 us (5%)
  between operations  14.1 us (4%)
    all_gather x1, waiting for transfers between devices, on_device(): summed = jnp.sum(lax.all_gather(partial_value, 'row'), axis=0)  102 us
    all_gather x1, waiting for transfers between devices, on_device(): lax.all_gather(filtered, 'col', axis=1, tiled=True)  52 us
    ppermute x12, waiting for transfers between devices, from_behind(): return lax.ppermute(block, axis, route)  33.7 us
    ppermute x12, starting transfers between devices, from_behind(): return lax.ppermute(block, axis, route)  30.7 us
    dot_general x3, matrix products, operate(): jnp.einsum('rqij,rqjk->rik', matrix_rows, gathered, preferred_element_typ...  27.4 us
    gather x3, local copies, waits for them, and re-layouts, operate(): gathered = jnp.concatenate([blocks[local_index], remote], axis=1)  26.4 us
    gather x3, local copies, waits for them, and re-layouts, fetch_remote(): return stacked[remote_index]  10.5 us
    concatenate x3, other arithmetic, fetch_remote(): jnp.concatenate([from_behind(blocks, 'row', -offset) for offset in offset...  8.01 us
  transfers between devices with their start and end apart: 14, of which 11 were waited for; matrix products, arithmetic and copies ran while one was open for 9% of the time, Pallas kernels for 0%

profile of v1, /device:TPU:1, one launch (start us, length us, event | category | flops | bytes accessed | tf_op | source)
XLA Modules:
  0.0 317.9 jit_solution(15542066978924452449)
XLA Ops:
  7.2 2.1 collective-permute-start.3
  9.3 2.1 collective-permute-start.2
  11.4 4.7 %collective-permute-start.1 = (bf16[24,128,128]{2,1,0:T(8,128)(2,1)}, bf16[24,128,128]{2,1,0:T(8,128)(2,1)S(1)}, u32[]{:S(2)}, u32[]{:S(2)}) collective-permute-start(bf16[24,128,128]{2,1,0:T(8,128)(2,1)} %bitcast.36), channel_id=1, source_target_pairs={{8,0},{12,4},{16,8},{20,12},{24,16},{28,20},{32,24},{36,28},{40,32... | collective-permute-start | bytes 2359304 | tf_op jit(solution)/shard_map/ppermute | solution.py:16
  16.1 1.0 collective-permute-start
  18.1 9.6 %gather_fusion = bf16[240,128,128]{2,1,0:T(8,128)(2,1)} fusion(bf16[24,128,128]{2,1,0:T(8,128)(2,1)} %bitcast.38, s32[1024]{0:T(1024)S(1)} %pad_clamp_fusion.1), kind=kCustom, calls=%fused_computation | custom fusion | bytes 15729600 | tf_op jit(solution)/shard_map/gather | solution.py:43
  27.7 5.7 %collective-permute-done.3 = bf16[24,128,128]{2,1,0:T(8,128)(2,1)S(1)} collective-permute-done((bf16[24,128,128]{2,1,0:T(8,128)(2,1)}, bf16[24,128,128]{2,1,0:T(8,128)(2,1)S(1)}, u32[]{:S(2)}, u32[]{:S(2)}) %collective-permute-start.3) | collective-permute-done | bytes 786464 | tf_op jit(solution)/shard_map/ppermute | solution.py:16
  33.4 2.1 collective-permute-done.2
  35.4 3.9 %collective-permute-done = bf16[24,128,128]{2,1,0:T(8,128)(2,1)S(1)} collective-permute-done((bf16[24,128,128]{2,1,0:T(8,128)(2,1)}, bf16[24,128,128]{2,1,0:T(8,128)(2,1)S(1)}, u32[]{:S(2)}, u32[]{:S(2)}) %collective-permute-start) | collective-permute-done | bytes 786464 | tf_op jit(solution)/shard_map/ppermute | solution.py:16
  39.4 1.9 pad_maximum_fusion
  41.3 2.8 gather_fusion.1
  44.1 8.5 %fusion.14 = bf16[24,128,128]{2,1,0:T(8,128)(2,1)S(1)} fusion(bf16[24,128,128]{2,1,0:T(8,128)(2,1)S(1)} %bitcast.39, bf16[24,12,128,128]{3,2,1,0:T(8,128)(2,1)} %bitcast.51, bf16[24,2,128,128]{3,2,1,0:T(8,128)(2,1)S(1)} %bitcast.49, bf16[24,10,128,128]{3,2,1,0:T(8,128)(2,1)} %bitcast.43), kind=kOutput, calls=%fused_computation.27 | convolution fusion | flops 1228800000 | bytes 20447232 | tf_op jit(solution)/shard_map/rqij,rqjk->rik/dot_general | solution.py:44
  53.5 7.7 %collective-permute-start.5 = (bf16[24,128,128]{2,1,0:T(8,128)(2,1)S(1)}, bf16[24,128,128]{2,1,0:T(8,128)(2,1)}, u32[]{:S(2)}, u32[]{:S(2)}) collective-permute-start(bf16[24,128,128]{2,1,0:T(8,128)(2,1)S(1)} %fusion.14), channel_id=1, source_target_pairs={{8,0},{12,4},{16,8},{20,12},{24,16},{28,20},{32,24},{36,28},{40,32... | collective-permute-start | bytes 2359304 | tf_op jit(solution)/shard_map/ppermute | solution.py:16
  61.8 8.4 %gather_fusion.2 = bf16[240,128,128]{2,1,0:T(8,128)(2,1)} fusion(bf16[24,128,128]{2,1,0:T(8,128)(2,1)S(1)} %fusion.14, s32[1024]{0:T(1024)S(1)} %pad_clamp_fusion.1), kind=kCustom, calls=%fused_computation.2 | custom fusion | bytes 15729600 | tf_op jit(solution)/shard_map/gather | solution.py:43
  70.2 7.6 %collective-permute-done.7 = bf16[24,128,128]{2,1,0:T(8,128)(2,1)S(1)} collective-permute-done((bf16[24,128,128]{2,1,0:T(8,128)(2,1)S(1)}, bf16[24,128,128]{2,1,0:T(8,128)(2,1)S(1)}, u32[]{:S(2)}, u32[]{:S(2)}) %collective-permute-start.7) | collective-permute-done | bytes 786464 | tf_op jit(solution)/shard_map/ppermute | solution.py:16
  77.8 1.2 collective-permute-done.6
  79.0 2.4 collective-permute-done.4
  81.4 3.0 pad_maximum_fusion.1
  84.5 3.9 %gather_fusion.3 = bf16[48,128,128]{2,1,0:T(8,128)(2,1)} fusion(bf16[96,128,128]{2,1,0:T(8,128)(2,1)} %pad_maximum_fusion.1, s32[1024]{0:T(1024)S(1)} %pad_clamp_fusion), kind=kCustom, calls=%fused_computation.3 | custom fusion | bytes 3145920 | tf_op jit(solution)/shard_map/gather | solution.py:39
  88.4 9.0 %fusion.15 = bf16[24,128,128]{2,1,0:T(8,128)(2,1)S(1)} fusion(bf16[24,128,128]{2,1,0:T(8,128)(2,1)S(1)} %bitcast.40, bf16[24,128,128]{2,1,0:T(8,128)(2,1)S(1)} %fusion.14, bf16[24,12,128,128]{3,2,1,0:T(8,128)(2,1)} %bitcast.52, bf16[24,2,128,128]{3,2,1,0:T(8,128)(2,1)} %bitcast.50, bf16[24,10,128,128]{3,2,1,0:T(8,128)(2,1)} %bitcast.44), kind=kOutput, calls=%fused_computation.28 | convolution fusion | flops 1229586432 | bytes 21233664 | tf_op jit(solution)/shard_map/rqij,rqjk->rik/dot_general | solution.py:44
  97.4 3.0 collective-permute-start.11
  100.4 8.1 %collective-permute-start.9 = (bf16[24,128,128]{2,1,0:T(8,128)(2,1)S(1)}, bf16[24,128,128]{2,1,0:T(8,128)(2,1)}, u32[]{:S(2)}, u32[]{:S(2)}) collective-permute-start(bf16[24,128,128]{2,1,0:T(8,128)(2,1)S(1)} %fusion.15), channel_id=1, source_target_pairs={{8,0},{12,4},{16,8},{20,12},{24,16},{28,20},{32,24},{36,28},{40,32... | collective-permute-start | bytes 2359304 | tf_op jit(solution)/shard_map/ppermute | solution.py:16
  109.2 8.4 %gather_fusion.4 = bf16[240,128,128]{2,1,0:T(8,128)(2,1)} fusion(bf16[24,128,128]{2,1,0:T(8,128)(2,1)S(1)} %fusion.15, s32[1024]{0:T(1024)S(1)} %pad_clamp_fusion.1), kind=kCustom, calls=%fused_computation.4 | custom fusion | bytes 15729600 | tf_op jit(solution)/shard_map/gather | solution.py:43
  117.6 8.3 %collective-permute-done.11 = bf16[24,128,128]{2,1,0:T(8,128)(2,1)S(1)} collective-permute-done((bf16[24,128,128]{2,1,0:T(8,128)(2,1)S(1)}, bf16[24,128,128]{2,1,0:T(8,128)(2,1)S(1)}, u32[]{:S(2)}, u32[]{:S(2)}) %collective-permute-start.11) | collective-permute-done | bytes 786464 | tf_op jit(solution)/shard_map/ppermute | solution.py:16
  126.2 2.2 collective-permute-done.8
  128.4 3.0 pad_maximum_fusion.2
  131.5 3.9 %gather_fusion.5 = bf16[48,128,128]{2,1,0:T(8,128)(2,1)} fusion(bf16[96,128,128]{2,1,0:T(8,128)(2,1)} %pad_maximum_fusion.2, s32[1024]{0:T(1024)S(1)} %pad_clamp_fusion), kind=kCustom, calls=%fused_computation.5 | custom fusion | bytes 3145920 | tf_op jit(solution)/shard_map/gather | solution.py:39
  135.3 9.9 %fusion.18 = bf16[24,128,128]{2,1,0:T(8,128)(2,1)} fusion(bf16[24,128,128]{2,1,0:T(8,128)(2,1)S(1)} %fusion.14, bf16[24,128,128]{2,1,0:T(8,128)(2,1)S(1)} %fusion.15, bf16[24,12,128,128]{3,2,1,0:T(8,128)(2,1)} %bitcast.53, bf16[24,2,128,128]{3,2,1,0:T(8,128)(2,1)} %bitcast.48, bf16[24,10,128,128]{3,2,1,0:T(8,128)(2,1)} %bitcast.42), kind=kOutput, calls=%fused_computation.31 | convolution fusion | flops 1229586432 | bytes 21233664 | tf_op jit(solution)/shard_map/rqij,rqjk->rik/dot_general | solution.py:44
  145.3 52.0 %all-gather.4.cloned.1.call-done = bf16[3072,512]{1,0:T(8,128)(2,1)} async-done(((bf16[3072,128]{1,0:T(8,128)(2,1)}), bf16[3072,512]{1,0:T(8,128)(2,1)}) %all-gather.4.cloned.1.call-update) | async-done | bytes 3145744 | tf_op jit(solution)/shard_map/all_gather | solution.py:62
  197.2 3.5 %fusion.32 = f32[128,512]{1,0:T(8,128)} fusion(bf16[3072,128]{1,0:T(8,128)(2,1)} %bitcast.46, bf16[3072,512]{1,0:T(8,128)(2,1)} %all-gather.4.cloned.1.call-done), kind=kOutput, calls=%fused_computation.51 | convolution fusion | flops 402653184 | bytes 4194304 | tf_op jit(solution)/shard_map/dot_general | solution.py:60
  200.7 102.1 %all-gather.6.cloned.1.call-done = f32[8192,512]{1,0:T(8,128)} async-done(((f32[128,512]{1,0:T(8,128)}), f32[8192,512]{1,0:T(8,128)}) %all-gather.6.cloned.1.call-update) | async-done | bytes 16777232 | tf_op jit(solution)/shard_map/all_gather | solution.py:66
  302.8 7.5 %reduce_sum.9 = f32[128,512]{1,0:T(8,128)S(1)} reduce(f32[64,128,512]{2,1,0:T(8,128)} %bitcast.41, f32[]{:T(128)} %constant.46.clone.1), dimensions={0}, to_apply=%region_0.1 | reduce | flops 4128768 | bytes 17039364 | tf_op jit(solution)/shard_map/reduce_sum | solution.py:66
  310.4 0.7 broadcast_multiply_fusion
  (24 shorter events, 3.5 us)
Async XLA Ops:
  7.2 190.1 %all-gather.4.cloned.1.call-start = ((), (), s32[]{:S(2)}) async-start(), calls=%async_computation | async-start | bytes 3932160 | tf_op jit(solution)/shard_map/all_gather | solution.py:62
  7.2 26.2 %collective-permute-start.3 = (bf16[24,128,128]{2,1,0:T(8,128)(2,1)}, bf16[24,128,128]{2,1,0:T(8,128)(2,1)S(1)}, u32[]{:S(2)}, u32[]{:S(2)}) collective-permute-start(bf16[24,128,128]{2,1,0:T(8,128)(2,1)} %bitcast.34), channel_id=1, source_target_pairs={{248,0},{252,4},{0,8},{4,12},{8,16},{12,20},{16,24},{20,28},{24,32... | collective-permute-start | bytes 2359304 | tf_op jit(solution)/shard_map/ppermute | solution.py:16
  9.3 26.1 %collective-permute-start.2 = (bf16[24,128,128]{2,1,0:T(8,128)(2,1)}, bf16[24,128,128]{2,1,0:T(8,128)(2,1)S(1)}, u32[]{:S(2)}, u32[]{:S(2)}) collective-permute-start(bf16[24,128,128]{2,1,0:T(8,128)(2,1)} %bitcast.35), channel_id=1, source_target_pairs={{252,0},{0,4},{4,8},{8,12},{12,16},{16,20},{20,24},{24,28},{28,32}... | collective-permute-start | bytes 2359304 | tf_op jit(solution)/shard_map/ppermute | solution.py:16
  11.4 24.1 %collective-permute-start.1 = (bf16[24,128,128]{2,1,0:T(8,128)(2,1)}, bf16[24,128,128]{2,1,0:T(8,128)(2,1)S(1)}, u32[]{:S(2)}, u32[]{:S(2)}) collective-permute-start(bf16[24,128,128]{2,1,0:T(8,128)(2,1)} %bitcast.36), channel_id=1, source_target_pairs={{8,0},{12,4},{16,8},{20,12},{24,16},{28,20},{32,24},{36,28},{40,32... | collective-permute-start | bytes 2359304 | tf_op jit(solution)/shard_map/ppermute | solution.py:16
  16.1 23.3 %collective-permute-start = (bf16[24,128,128]{2,1,0:T(8,128)(2,1)}, bf16[24,128,128]{2,1,0:T(8,128)(2,1)S(1)}, u32[]{:S(2)}, u32[]{:S(2)}) collective-permute-start(bf16[24,128,128]{2,1,0:T(8,128)(2,1)} %bitcast.37), channel_id=1, source_target_pairs={{4,0},{8,4},{12,8},{16,12},{20,16},{24,20},{28,24},{32,28},{36,32}... | collective-permute-start | bytes 2359304 | tf_op jit(solution)/shard_map/ppermute | solution.py:16
  41.3 2.8 copy-start
  52.7 25.1 %collective-permute-start.7 = (bf16[24,128,128]{2,1,0:T(8,128)(2,1)S(1)}, bf16[24,128,128]{2,1,0:T(8,128)(2,1)S(1)}, u32[]{:S(2)}, u32[]{:S(2)}) collective-permute-start(bf16[24,128,128]{2,1,0:T(8,128)(2,1)S(1)} %fusion.14), channel_id=1, source_target_pairs={{248,0},{252,4},{0,8},{4,12},{8,16},{12,20},{16,24},{20,28},{24,32... | collective-permute-start | bytes 2359304 | tf_op jit(solution)/shard_map/ppermute | solution.py:16
  53.2 25.8 %collective-permute-start.6 = (bf16[24,128,128]{2,1,0:T(8,128)(2,1)S(1)}, bf16[24,128,128]{2,1,0:T(8,128)(2,1)S(1)}, u32[]{:S(2)}, u32[]{:S(2)}) collective-permute-start(bf16[24,128,128]{2,1,0:T(8,128)(2,1)S(1)} %fusion.14), channel_id=1, source_target_pairs={{252,0},{0,4},{4,8},{8,12},{12,16},{16,20},{20,24},{24,28},{28,32}... | collective-permute-start | bytes 2359304 | tf_op jit(solution)/shard_map/ppermute | solution.py:16
  53.5 25.6 %collective-permute-start.5 = (bf16[24,128,128]{2,1,0:T(8,128)(2,1)S(1)}, bf16[24,128,128]{2,1,0:T(8,128)(2,1)}, u32[]{:S(2)}, u32[]{:S(2)}) collective-permute-start(bf16[24,128,128]{2,1,0:T(8,128)(2,1)S(1)} %fusion.14), channel_id=1, source_target_pairs={{8,0},{12,4},{16,8},{20,12},{24,16},{28,20},{32,24},{36,28},{40,32... | collective-permute-start | bytes 2359304 | tf_op jit(solution)/shard_map/ppermute | solution.py:16
  61.2 20.3 %collective-permute-start.4 = (bf16[24,128,128]{2,1,0:T(8,128)(2,1)S(1)}, bf16[24,128,128]{2,1,0:T(8,128)(2,1)}, u32[]{:S(2)}, u32[]{:S(2)}) collective-permute-start(bf16[24,128,128]{2,1,0:T(8,128)(2,1)S(1)} %fusion.14), channel_id=1, source_target_pairs={{4,0},{8,4},{12,8},{16,12},{20,16},{24,20},{28,24},{32,28},{36,32}... | collective-permute-start | bytes 2359304 | tf_op jit(solution)/shard_map/ppermute | solution.py:16
  97.4 28.5 %collective-permute-start.11 = (bf16[24,128,128]{2,1,0:T(8,128)(2,1)S(1)}, bf16[24,128,128]{2,1,0:T(8,128)(2,1)S(1)}, u32[]{:S(2)}, u32[]{:S(2)}) collective-permute-start(bf16[24,128,128]{2,1,0:T(8,128)(2,1)S(1)} %fusion.15), channel_id=1, source_target_pairs={{248,0},{252,4},{0,8},{4,12},{8,16},{12,20},{16,24},{20,28},{24,32... | collective-permute-start | bytes 2359304 | tf_op jit(solution)/shard_map/ppermute | solution.py:16
  100.4 25.8 %collective-permute-start.10 = (bf16[24,128,128]{2,1,0:T(8,128)(2,1)S(1)}, bf16[24,128,128]{2,1,0:T(8,128)(2,1)S(1)}, u32[]{:S(2)}, u32[]{:S(2)}) collective-permute-start(bf16[24,128,128]{2,1,0:T(8,128)(2,1)S(1)} %fusion.15), channel_id=1, source_target_pairs={{252,0},{0,4},{4,8},{8,12},{12,16},{16,20},{20,24},{24,28},{28,32}... | collective-permute-start | bytes 2359304 | tf_op jit(solution)/shard_map/ppermute | solution.py:16
  100.4 25.8 %collective-permute-start.9 = (bf16[24,128,128]{2,1,0:T(8,128)(2,1)S(1)}, bf16[24,128,128]{2,1,0:T(8,128)(2,1)}, u32[]{:S(2)}, u32[]{:S(2)}) collective-permute-start(bf16[24,128,128]{2,1,0:T(8,128)(2,1)S(1)} %fusion.15), channel_id=1, source_target_pairs={{8,0},{12,4},{16,8},{20,12},{24,16},{28,20},{32,24},{36,28},{40,32... | collective-permute-start | bytes 2359304 | tf_op jit(solution)/shard_map/ppermute | solution.py:16
  108.5 19.9 %collective-permute-start.8 = (bf16[24,128,128]{2,1,0:T(8,128)(2,1)S(1)}, bf16[24,128,128]{2,1,0:T(8,128)(2,1)}, u32[]{:S(2)}, u32[]{:S(2)}) collective-permute-start(bf16[24,128,128]{2,1,0:T(8,128)(2,1)S(1)} %fusion.15), channel_id=1, source_target_pairs={{4,0},{8,4},{12,8},{16,12},{20,16},{24,20},{28,24},{32,28},{36,32}... | collective-permute-start | bytes 2359304 | tf_op jit(solution)/shard_map/ppermute | solution.py:16
  145.2 157.6 %all-gather.6.cloned.1.call-start = ((), (), s32[]{:S(2)}) async-start(), calls=%async_computation.1 | async-start | bytes 17039360 | tf_op jit(solution)/shard_map/all_gather | solution.py:66
Sparse Core Ops, SparseCore 0:
  145.4 51.8 all-gather.3
  200.8 101.9 all-gather.5
